TPU v7x, 512 devices: a whole 4x4x16 slice. The times are simulated.
512 devices in a mesh: day: 64 (over z, y), pair: 8 (over x, core).
Axes of the slice: x: 4, y: 4, z: 16, core: 2. Of those that a mesh axis runs over, the one named last changes fastest.
Arguments:
- spectra: bfloat16 [128, 128, 4096], P('day', 'pair'), may hold values from -40 to 40
- pair_stations: int32 [512, 2], P('pair'), may hold values from 0 to 127
- availability: int32 [128, 128], P('day'), may hold values from 0 to 1
Outputs:
- stacks: bfloat16 [128, 512, 1001], P('day', 'pair')
- reference: float32 [512, 1001], P('pair')
All inputs are finite; a program needn't handle non-finite values.
Results may differ from a plain program's by a relative error of at most 0.008.
Values may be sent and summed in bfloat16 or wider, within the bound.
A program may use at most 64 MiB of HBM per device.

v0:
```python
import jax
import jax.numpy as jnp
import numpy as np
from jax import lax
from jax.sharding import PartitionSpec as P

LAGS = 1001
WIDE = 1024
WINDOW = 30


def lag_table(bin_count):
    bin_ids = np.arange(bin_count)[:, None]
    lag_ids = np.arange(LAGS)[None, :] - (LAGS - 1) // 2
    angle = np.mod(bin_ids * lag_ids, 2 * bin_count) * (np.pi / bin_count)
    factor = 1.0 / np.sqrt(2.0 * bin_count)
    table = np.concatenate([np.cos(angle) * factor, -np.sin(angle) * factor], 0)
    return np.pad(table, ((0, 0), (0, WIDE - LAGS))).astype(np.float32).astype(jnp.bfloat16)


def per_device(spectra, pair_stations, availability):
    days_here = spectra.shape[0]
    groups = lax.axis_size("day")
    station_count = spectra.shape[1] * lax.axis_size("pair")
    bin_count = spectra.shape[2] // 2
    pairs_here = pair_stations.shape[0]
    inverse = jnp.asarray(lag_table(bin_count))
    station_ids = jnp.arange(station_count, dtype=jnp.int32)
    ends = jnp.concatenate([pair_stations[:, 0], pair_stations[:, 1]], 0)
    pick = (ends[:, None] == station_ids[None, :]).astype(jnp.bfloat16)
    avail = jnp.dot(availability.astype(jnp.bfloat16), pick.T, preferred_element_type=jnp.float32)
    present = avail[:, :pairs_here] * avail[:, pairs_here:]
    gathered = lax.all_gather(spectra, "pair", axis=1, tiled=True)
    rows = []
    for day in range(days_here):
        spec = jnp.dot(pick, gathered[day], preferred_element_type=jnp.float32)
        one, two = (spec[:pairs_here], spec[pairs_here:])
        ar, ai, br, bi = (
            one[:, :bin_count],
            one[:, bin_count:],
            two[:, :bin_count],
            two[:, bin_count:],
        )
        rows.append(jnp.concatenate([ar * br + ai * bi, ar * bi - ai * br], 1).astype(jnp.bfloat16))
    cross = jnp.concatenate(rows, 0)
    corr = jnp.dot(cross, inverse, preferred_element_type=jnp.float32)
    column = lax.broadcasted_iota(jnp.int32, (1, WIDE), 1)
    shown = present.reshape(-1, 1)
    daily = jnp.where(column == LAGS, shown, corr * shown).astype(jnp.bfloat16)
    daily = daily.reshape(days_here, pairs_here, WIDE)
    turned = lax.all_to_all(daily, "day", split_axis=1, concat_axis=0, tiled=True)
    days = groups * days_here
    mine = turned.reshape(days, WIDE)
    day_ids = np.arange(days)
    gap = day_ids[:, None] - day_ids[None, :]
    band = jnp.asarray(((gap >= 0) & (gap < WINDOW)).astype(np.float32), dtype=jnp.bfloat16)
    moving = jnp.dot(band, mine, preferred_element_type=jnp.float32)
    counts = moving[:, LAGS : LAGS + 1]
    ref = jnp.sum(mine.astype(jnp.float32), axis=0) / days
    ref = jnp.where(column[0] < LAGS, ref, 0.0)
    scale = jnp.sqrt(jnp.sum(ref * ref) / LAGS + 1e-06)
    stacks = (moving / jnp.maximum(counts, 1.0) / scale).astype(jnp.bfloat16)
    back = lax.all_to_all(
        stacks.reshape(days, 1, WIDE), "day", split_axis=0, concat_axis=1, tiled=True
    )
    ref_all = lax.all_gather(ref[None], "day", axis=0, tiled=True)
    return (back[:, :, :LAGS], ref_all[:, :LAGS])


def solution(mesh):
    return jax.shard_map(
        per_device,
        mesh=mesh,
        in_specs=(P("day", "pair", None), P("pair", None), P("day", None)),
        out_specs=(P("day", "pair", None), P("pair", None)),
        check_vma=False,
    )
```

profile of v0, /device:TPU:8, one launch (start us, length us, event | category | flops | bytes accessed | tf_op | source)
XLA Modules:
  0.0 198.5 jit_solution(13838983268094882941)
XLA Ops:
  7.2 0.7 all-gather.3.cloned.1.call-update
  7.9 0.8 slice_bitcast_fusion.5
  8.7 0.9 convolution_bitcast_fusion
  9.8 37.6 %all-gather.3.cloned.1.call-done = bf16[2,128,4096]{2,1,0:T(8,128)(2,1)} async-done(((bf16[2,16,4096]{2,1,0:T(8,128)(2,1)}), bf16[2,128,4096]{2,1,0:T(8,128)(2,1)}) %all-gather.3.cloned.1.call-update) | async-done | bytes 2097168 | tf_op jit(solution)/shard_map/all_gather | solution.py:33
  47.4 1.8 fusion.3
  49.3 0.5 fusion.2
  49.8 0.4 add_convert_fusion
  50.2 2.5 %copy-done.2 = bf16[4096,1024]{1,0:T(8,128)(2,1)S(1)} copy-done((bf16[4096,1024]{1,0:T(8,128)(2,1)S(1)}, bf16[4096,1024]{1,0:T(8,128)(2,1)}, u32[]{:S(2)}) %copy-start.2) | copy-done | bytes 8388632
  52.7 1.3 fusion.1
  54.0 0.3 copy.12
  54.3 37.4 %all_to_all.33 = bf16[2,64,1024]{2,0,1:T(2,128)(2,1)S(1)} all-to-all(bf16[2,64,1024]{2,0,1:T(2,128)(2,1)S(1)} %copy.12), channel_id=1, replica_groups=mesh['day'=64,'pair'=8] {'day'}, dimensions={1} | all-to-all | bytes 524288 | tf_op jit(solution)/shard_map/all_to_all | solution.py:51
  91.7 0.2 convert_reduce_fusion
  91.9 0.6 broadcast_multiply_fusion
  93.3 0.2 fusion.18
  93.5 0.2 fusion.11
  93.8 0.5 broadcast.36
  94.3 0.8 reduce.6
  95.1 0.8 reshape.58
  95.9 5.9 %all-to-all-start.1 = ((bf16[64,2,1024]{2,1,0:T(2,128)(2,1)}), bf16[64,2,1024]{2,1,0:T(2,128)(2,1)S(1)}, u32[]{:S(2)}, u32[]{:S(2)}) async-start(bf16[64,2,1024]{2,1,0:T(2,128)(2,1)} %reshape.58), calls=%async_computation.1 | async-start | bytes 524288 | tf_op jit(solution)/shard_map/all_to_all | solution.py:63
  101.9 86.4 %all-gather = f32[64,1,1024]{2,1,0:T(1,128)S(1)} all-gather(f32[1,1,1024]{2,1,0:T(1,128)S(1)} %fusion.15), channel_id=1, replica_groups=mesh['day'=64,'pair'=8] {'day'}, dimensions={0}, use_global_device_ids=true | all-gather | bytes 266240 | tf_op jit(solution)/shard_map/all_gather | solution.py:66
  188.3 0.8 copy.19
  189.1 0.2 reshape.59
  189.3 1.5 reduce.4
  190.9 0.8 copy.15
  (15 shorter events, 0.6 us)
Async XLA Ops:
  7.2 40.2 %all-gather.3.cloned.1.call-start = ((), (), s32[]{:S(2)}) async-start(), calls=%async_computation.2 | async-start | bytes 2359296 | tf_op jit(solution)/shard_map/all_gather | solution.py:33
  47.4 1.9 copy-start
  49.3 3.4 %copy-start.2 = (bf16[4096,1024]{1,0:T(8,128)(2,1)S(1)}, bf16[4096,1024]{1,0:T(8,128)(2,1)}, u32[]{:S(2)}) copy-start(bf16[4096,1024]{1,0:T(8,128)(2,1)} %constant.19.clone) | copy-start | bytes 25165828
  52.7 40.6 %copy-start.1 = (bf16[128,128]{1,0:T(8,128)(2,1)S(1)}, bf16[128,128]{1,0:T(8,128)(2,1)}, u32[]{:S(2)}) copy-start(bf16[128,128]{1,0:T(8,128)(2,1)} %constant.25) | copy-start | bytes 98308
  95.9 93.1 %all-to-all-start.1 = ((bf16[64,2,1024]{2,1,0:T(2,128)(2,1)}), bf16[64,2,1024]{2,1,0:T(2,128)(2,1)S(1)}, u32[]{:S(2)}, u32[]{:S(2)}) async-start(bf16[64,2,1024]{2,1,0:T(2,128)(2,1)} %reshape.58), calls=%async_computation.1 | async-start | bytes 524288 | tf_op jit(solution)/shard_map/all_to_all | solution.py:63
Sparse Core Ops, SparseCore 0:
  10.1 37.1 all-gather.2
where the time goes:
time: 199 us
  blocking collectives  124 us (62%)
  waiting for transfers between devices  38.3 us (19%)
  between operations  14.8 us (7%)
  local copies, waits for them, and re-layouts  6.83 us (3%)
  starting transfers between devices  5.97 us (3%)
  matrix products  4.73 us (2%)
  other arithmetic  4.04 us (2%)
    all_gather x1, blocking collectives, per_device(): ref_all = lax.all_gather(ref[None], 'day', axis=0, tiled=True)  86.4 us
    all_gather x1, waiting for transfers between devices, per_device(): gathered = lax.all_gather(spectra, 'pair', axis=1, tiled=True)  37.6 us
    all_to_all x1, blocking collectives, per_device(): lax.all_to_all(daily, 'day', split_axis=1, concat_axis=0, tiled=True)  37.4 us
    all_to_all x1, starting transfers between devices, per_device(): lax.all_to_all(stacks.reshape(days, 1, WIDE), 'day', split_axis=0, concat...  5.93 us
    unnamed x10, local copies, waits for them, and re-layouts  5.05 us
  transfers between devices with their start and end apart: 2, of which 1 were waited for; matrix products, arithmetic and copies ran while one was open for 1% of the time, Pallas kernels for 0%

commit v1 on v0

--- a/solution.py
+++ b/solution.py
@@ -7,6 +7,18 @@
 LAGS = 1001
 WIDE = 1024
 WINDOW = 30
+
+
+def open_the_lane(chunk):
+    num_devices = lax.axis_size("pair")
+    log = [(no, (no + 1) % num_devices) for no in range(num_devices)]
+    carry = [None] * num_devices
+    carry[num_devices - 1] = chunk
+    for m in range(num_devices - 2, -1, -1):
+        carry[m] = lax.ppermute(carry[m + 1], "pair", log)
+    x_now = jnp.concatenate(carry, axis=1)
+    w_next = (lax.axis_index("pair") + 1) * chunk.shape[1]
+    return jnp.roll(x_now, w_next, axis=1)
 
 
 def lag_table(bin_count):
@@ -30,7 +42,7 @@
     pick = (ends[:, None] == station_ids[None, :]).astype(jnp.bfloat16)
     avail = jnp.dot(availability.astype(jnp.bfloat16), pick.T, preferred_element_type=jnp.float32)
     present = avail[:, :pairs_here] * avail[:, pairs_here:]
-    gathered = lax.all_gather(spectra, "pair", axis=1, tiled=True)
+    gathered = open_the_lane(spectra)
     rows = []
     for day in range(days_here):
         spec = jnp.dot(pick, gathered[day], preferred_element_type=jnp.float32)

time: 199 us -> 189 us (0.950)
  between operations: 14.8 us -> 1.61 us
  waiting for transfers between devices: 38.3 us -> 47.4 us
  blocking collectives: 124 us -> 119 us
    ppermute x0 -> x7, waiting for transfers between devices: none -> 47.4 us  [open_the_lane(): carry[m] = lax.ppermute(carry[m + 1], 'pair', log)]
    all_gather x1 -> x0, waiting for transfers between devices: 37.6 us -> none  [per_device(): gathered = lax.all_gather(spectra, 'pair', axis=1, tiled=True)]
    all_gather x1, blocking collectives: 86.4 us -> 82.9 us  [per_device(): ref_all = lax.all_gather(ref[None], 'day', axis=0, tiled=True)]
    unnamed x10 -> x27, local copies, waits for them, and re-layouts: 5.05 us -> 5.78 us
  transfers between devices with their start and end apart: 2 -> 8, of which waited for: 1 -> 7; matrix products, arithmetic and copies ran while one was open for 1% -> 1% of each run, Pallas kernels for 0% -> 0%
where the time goes in v1:
time: 189 us
  blocking collectives  119 us (63%)
  waiting for transfers between devices  47.4 us (25%)
  local copies, waits for them, and re-layouts  7.58 us (4%)
  starting transfers between devices  5.75 us (3%)
  other arithmetic  4.03 us (2%)
  matrix products  3.36 us (2%)
    all_gather x1, blocking collectives, per_device(): ref_all = lax.all_gather(ref[None], 'day', axis=0, tiled=True)  82.9 us
    ppermute x7, waiting for transfers between devices, open_the_lane(): carry[m] = lax.ppermute(carry[m + 1], 'pair', log)  47.4 us
    all_to_all x1, blocking collectives, per_device(): lax.all_to_all(daily, 'day', split_axis=1, concat_axis=0, tiled=True)  36 us
    unnamed x27, local copies, waits for them, and re-layouts  5.78 us
    all_to_all x1, starting transfers between devices, per_device(): lax.all_to_all(stacks.reshape(days, 1, WIDE), 'day', split_axis=0, concat...  5.71 us
  transfers between devices with their start and end apart: 8, of which 7 were waited for; matrix products, arithmetic and copies ran while one was open for 1% of the time, Pallas kernels for 0%

profile of v1, /device:TPU:8, one launch (start us, length us, event | category | flops | bytes accessed | tf_op | source)
XLA Modules:
  0.0 188.6 jit_solution(9228744218664644967)
XLA Ops:
  0.7 7.2 %collective-permute-done = bf16[2,16,4096]{2,1,0:T(8,128)(2,1)S(1)} collective-permute-done((bf16[2,16,4096]{2,1,0:T(8,128)(2,1)}, bf16[2,16,4096]{2,1,0:T(8,128)(2,1)S(1)}, u32[]{:S(2)}, u32[]{:S(2)}) %collective-permute-start) | collective-permute-done | bytes 262176 | tf_op jit(solution)/shard_map/ppermute | solution.py:18
  7.9 7.0 %collective-permute-done.1 = bf16[2,16,4096]{2,1,0:T(8,128)(2,1)S(1)} collective-permute-done((bf16[2,16,4096]{2,1,0:T(8,128)(2,1)S(1)}, bf16[2,16,4096]{2,1,0:T(8,128)(2,1)S(1)}, u32[]{:S(2)}, u32[]{:S(2)}) %collective-permute-start.1) | collective-permute-done | bytes 262176 | tf_op jit(solution)/shard_map/ppermute | solution.py:18
  14.9 7.0 %collective-permute-done.2 = bf16[2,16,4096]{2,1,0:T(8,128)(2,1)S(1)} collective-permute-done((bf16[2,16,4096]{2,1,0:T(8,128)(2,1)S(1)}, bf16[2,16,4096]{2,1,0:T(8,128)(2,1)S(1)}, u32[]{:S(2)}, u32[]{:S(2)}) %collective-permute-start.2) | collective-permute-done | bytes 262176 | tf_op jit(solution)/shard_map/ppermute | solution.py:18
  21.9 7.0 %collective-permute-done.3 = bf16[2,16,4096]{2,1,0:T(8,128)(2,1)S(1)} collective-permute-done((bf16[2,16,4096]{2,1,0:T(8,128)(2,1)S(1)}, bf16[2,16,4096]{2,1,0:T(8,128)(2,1)S(1)}, u32[]{:S(2)}, u32[]{:S(2)}) %collective-permute-start.3) | collective-permute-done | bytes 262176 | tf_op jit(solution)/shard_map/ppermute | solution.py:18
  28.9 0.8 slice_bitcast_fusion.1
  29.7 6.2 %collective-permute-done.4 = bf16[2,16,4096]{2,1,0:T(8,128)(2,1)S(1)} collective-permute-done((bf16[2,16,4096]{2,1,0:T(8,128)(2,1)S(1)}, bf16[2,16,4096]{2,1,0:T(8,128)(2,1)S(1)}, u32[]{:S(2)}, u32[]{:S(2)}) %collective-permute-start.4) | collective-permute-done | bytes 262176 | tf_op jit(solution)/shard_map/ppermute | solution.py:18
  36.0 0.9 convolution_bitcast_fusion
  36.9 6.1 %collective-permute-done.5 = bf16[2,16,4096]{2,1,0:T(8,128)(2,1)S(1)} collective-permute-done((bf16[2,16,4096]{2,1,0:T(8,128)(2,1)S(1)}, bf16[2,16,4096]{2,1,0:T(8,128)(2,1)S(1)}, u32[]{:S(2)}, u32[]{:S(2)}) %collective-permute-start.5) | collective-permute-done | bytes 262176 | tf_op jit(solution)/shard_map/ppermute | solution.py:18
  43.1 6.8 %collective-permute-done.6 = bf16[2,16,4096]{2,1,0:T(8,128)(2,1)S(1)} collective-permute-done((bf16[2,16,4096]{2,1,0:T(8,128)(2,1)S(1)}, bf16[2,16,4096]{2,1,0:T(8,128)(2,1)S(1)}, u32[]{:S(2)}, u32[]{:S(2)}) %collective-permute-start.6) | collective-permute-done | bytes 262176 | tf_op jit(solution)/shard_map/ppermute | solution.py:18
  50.1 1.0 constant_dynamic-update-slice_fusion.8
  51.3 0.5 fusion.3
  52.8 0.5 slice-done
  53.3 1.5 slice-done.1
  54.8 1.3 fusion.1
  56.4 36.0 %all_to_all.33 = bf16[2,64,1024]{2,0,1:T(2,128)(2,1)S(1)} all-to-all(bf16[2,64,1024]{2,0,1:T(2,128)(2,1)S(1)} %copy.12), channel_id=1, replica_groups=mesh['day'=64,'pair'=8] {'day'}, dimensions={1} | all-to-all | bytes 524288 | tf_op jit(solution)/shard_map/all_to_all | solution.py:63
  92.6 0.6 broadcast_multiply_fusion
  94.5 0.5 broadcast.37
  95.0 0.8 reduce.6
  95.8 0.8 reshape.58
  96.6 5.7 %all-to-all-start.1 = ((bf16[64,2,1024]{2,1,0:T(2,128)(2,1)}), bf16[64,2,1024]{2,1,0:T(2,128)(2,1)S(1)}, u32[]{:S(2)}, u32[]{:S(2)}) async-start(bf16[64,2,1024]{2,1,0:T(2,128)(2,1)} %reshape.58), calls=%async_computation.1 | async-start | bytes 524288 | tf_op jit(solution)/shard_map/all_to_all | solution.py:75
  102.4 82.9 %all-gather = f32[64,1,1024]{2,1,0:T(1,128)S(1)} all-gather(f32[1,1,1024]{2,1,0:T(1,128)S(1)} %fusion.15), channel_id=1, replica_groups=mesh['day'=64,'pair'=8] {'day'}, dimensions={0}, use_global_device_ids=true | all-gather | bytes 266240 | tf_op jit(solution)/shard_map/all_gather | solution.py:78
  185.3 0.8 copy.19
  186.3 1.5 reduce.4
  187.9 0.8 copy.15
  (45 shorter events, 2.9 us)
Async XLA Ops:
  0.6 50.7 %copy-start = (bf16[2,16,4096]{2,1,0:T(8,128)(2,1)S(1)}, bf16[2,16,4096]{2,1,0:T(8,128)(2,1)}, u32[]{:S(2)}) copy-start(bf16[2,16,4096]{2,1,0:T(8,128)(2,1)} %param.5) | copy-start | bytes 786436
  0.6 7.2 %collective-permute-start = (bf16[2,16,4096]{2,1,0:T(8,128)(2,1)}, bf16[2,16,4096]{2,1,0:T(8,128)(2,1)S(1)}, u32[]{:S(2)}, u32[]{:S(2)}) collective-permute-start(bf16[2,16,4096]{2,1,0:T(8,128)(2,1)} %param.5), channel_id=1, source_target_pairs={{0,1},{1,2},{2,3},{3,4},{4,5},{5,6},{6,7},{7,0},{8,9},{9,10},{10,1... | collective-permute-start | bytes 786440 | tf_op jit(solution)/shard_map/ppermute | solution.py:18
  7.9 7.0 %collective-permute-start.1 = (bf16[2,16,4096]{2,1,0:T(8,128)(2,1)S(1)}, bf16[2,16,4096]{2,1,0:T(8,128)(2,1)S(1)}, u32[]{:S(2)}, u32[]{:S(2)}) collective-permute-start(bf16[2,16,4096]{2,1,0:T(8,128)(2,1)S(1)} %collective-permute-done), channel_id=1, source_target_pairs={{0,1},{1,2},{2,3},{3,4},{4,5},{5,6},{6,7},{7,0},{8,9},{9,10},{10,1... | collective-permute-start | bytes 786440 | tf_op jit(solution)/shard_map/ppermute | solution.py:18
  14.9 7.0 %collective-permute-start.2 = (bf16[2,16,4096]{2,1,0:T(8,128)(2,1)S(1)}, bf16[2,16,4096]{2,1,0:T(8,128)(2,1)S(1)}, u32[]{:S(2)}, u32[]{:S(2)}) collective-permute-start(bf16[2,16,4096]{2,1,0:T(8,128)(2,1)S(1)} %collective-permute-done.1), channel_id=1, source_target_pairs={{0,1},{1,2},{2,3},{3,4},{4,5},{5,6},{6,7},{7,0},{8,9},{9,10},{10,1... | collective-permute-start | bytes 786440 | tf_op jit(solution)/shard_map/ppermute | solution.py:18
  21.9 7.0 %collective-permute-start.3 = (bf16[2,16,4096]{2,1,0:T(8,128)(2,1)S(1)}, bf16[2,16,4096]{2,1,0:T(8,128)(2,1)S(1)}, u32[]{:S(2)}, u32[]{:S(2)}) collective-permute-start(bf16[2,16,4096]{2,1,0:T(8,128)(2,1)S(1)} %collective-permute-done.2), channel_id=1, source_target_pairs={{0,1},{1,2},{2,3},{3,4},{4,5},{5,6},{6,7},{7,0},{8,9},{9,10},{10,1... | collective-permute-start | bytes 786440 | tf_op jit(solution)/shard_map/ppermute | solution.py:18
  28.9 7.0 %collective-permute-start.4 = (bf16[2,16,4096]{2,1,0:T(8,128)(2,1)S(1)}, bf16[2,16,4096]{2,1,0:T(8,128)(2,1)S(1)}, u32[]{:S(2)}, u32[]{:S(2)}) collective-permute-start(bf16[2,16,4096]{2,1,0:T(8,128)(2,1)S(1)} %collective-permute-done.3), channel_id=1, source_target_pairs={{0,1},{1,2},{2,3},{3,4},{4,5},{5,6},{6,7},{7,0},{8,9},{9,10},{10,1... | collective-permute-start | bytes 786440 | tf_op jit(solution)/shard_map/ppermute | solution.py:18
  35.9 7.0 %collective-permute-start.5 = (bf16[2,16,4096]{2,1,0:T(8,128)(2,1)S(1)}, bf16[2,16,4096]{2,1,0:T(8,128)(2,1)S(1)}, u32[]{:S(2)}, u32[]{:S(2)}) collective-permute-start(bf16[2,16,4096]{2,1,0:T(8,128)(2,1)S(1)} %collective-permute-done.4), channel_id=1, source_target_pairs={{0,1},{1,2},{2,3},{3,4},{4,5},{5,6},{6,7},{7,0},{8,9},{9,10},{10,1... | collective-permute-start | bytes 786440 | tf_op jit(solution)/shard_map/ppermute | solution.py:18
  42.9 7.0 %collective-permute-start.6 = (bf16[2,16,4096]{2,1,0:T(8,128)(2,1)S(1)}, bf16[2,16,4096]{2,1,0:T(8,128)(2,1)S(1)}, u32[]{:S(2)}, u32[]{:S(2)}) collective-permute-start(bf16[2,16,4096]{2,1,0:T(8,128)(2,1)S(1)} %collective-permute-done.5), channel_id=1, source_target_pairs={{0,1},{1,2},{2,3},{3,4},{4,5},{5,6},{6,7},{7,0},{8,9},{9,10},{10,1... | collective-permute-start | bytes 786440 | tf_op jit(solution)/shard_map/ppermute | solution.py:18
  51.1 2.2 %slice-start = ((s8[8388608]{0:T(1024)(128)(4,1)}), s8[4194304]{0:T(1024)(128)(4,1)S(1)}, s32[]{:S(2)}) async-start(s8[8388608]{0:T(1024)(128)(4,1)} %bitcast.35), calls=%async_computation.2 | async-start | bytes 8388608
  51.8 2.9 %slice-start.1 = ((s8[8388608]{0:T(1024)(128)(4,1)}), s8[4194304]{0:T(1024)(128)(4,1)S(1)}, s32[]{:S(2)}) async-start(s8[8388608]{0:T(1024)(128)(4,1)} %bitcast.35), calls=%async_computation.3 | async-start | bytes 8388608
  54.8 39.2 %copy-start.1 = (bf16[128,128]{1,0:T(8,128)(2,1)S(1)}, bf16[128,128]{1,0:T(8,128)(2,1)}, u32[]{:S(2)}) copy-start(bf16[128,128]{1,0:T(8,128)(2,1)} %constant.55) | copy-start | bytes 98308
  96.6 89.4 %all-to-all-start.1 = ((bf16[64,2,1024]{2,1,0:T(2,128)(2,1)}), bf16[64,2,1024]{2,1,0:T(2,128)(2,1)S(1)}, u32[]{:S(2)}, u32[]{:S(2)}) async-start(bf16[64,2,1024]{2,1,0:T(2,128)(2,1)} %reshape.58), calls=%async_computation.1 | async-start | bytes 524288 | tf_op jit(solution)/shard_map/all_to_all | solution.py:75
